TPU v7x, 32 devices: a whole 2x2x4 slice. The times are simulated.
32 devices in a mesh: parts: 1, leaf: 32 (over z, y, x, core).
Axes of the slice: x: 2, y: 2, z: 4, core: 2. Of those that a mesh axis runs over, the one named last changes fastest.
Arguments:
- points: bfloat16 [640, 8, 256], P(('parts', 'leaf')), may hold values from -3 to 6
- charges: bfloat16 [640, 32, 256], P(('parts', 'leaf')), may hold values from -0.625 to 0.625
- basis: bfloat16 [640, 256, 128], P(('parts', 'leaf')), may hold values from -0.375 to 0.375
- transfer: bfloat16 [640, 128, 128], P(('parts', 'leaf')), may hold values from -0.5 to 0.5
- skeleton: bfloat16 [640, 8, 128], P(('parts', 'leaf')), may hold values from -3 to 6
- top_skeleton: bfloat16 [16, 8, 128], P('parts'), may hold values from -5 to 8
- near_mask: int32 [640, 14], P(('parts', 'leaf')), may hold values 0 or 1
- remote_dev: int32 [640, 12], P(('parts', 'leaf')), may hold values from 0 to 30, all different within a row; in each aligned block of 20 rows (0 to 19, 20 to 39, ...) at most 9 rows name the same one
- remote_leaf: int32 [640, 12], P(('parts', 'leaf')), may hold values from 0 to 19
- far_mask: int32 [640, 6], P(('parts', 'leaf')), may hold values 0 or 1
- top_far: int32 [16, 8], P('parts'), may hold values from 0 to 15, as said below
Outputs:
- product: float32 [640, 32, 256], P(('parts', 'leaf'))
Inputs may be any that keep to these rules, and one draw needn't show every extreme that they name: `remote_dev`: each row names 12 different values; the 20 rows of one device name any value at most 9 times, a bound that some block reaches. `top_far`: each row names 8 different nodes, never its own.
All inputs are finite; a program needn't handle non-finite values. No bound on the sum of `near_mask` or of `far_mask` on one device may be relied on, other than what follows from the above.
Results may differ from a plain program's by a relative error of at most 0.0039.
Values may be sent and summed in bfloat16 or wider, within the bound.
A program may use at most 64 MiB of HBM per device.

v0:
```python
import math

import jax
import jax.numpy as jnp
from jax import lax
from jax.sharding import PartitionSpec as P

ROOT_THREE = math.sqrt(3.0)
LENGTH_SCALE = 1.0


def with_halo(array, sides, width):
    for axis, dim in sides:
        count, length = (lax.axis_size(axis), array.shape[dim])
        up = [(i, (i + 1) % count) for i in range(count - 1)]
        down = [(j, i) for i, j in up]
        last = lax.slice_in_dim(array, length - width, length, axis=dim)
        initial = lax.slice_in_dim(array, 0, width, axis=dim)
        before = lax.ppermute(last, axis, up)
        after = lax.ppermute(initial, axis, down)
        array = jnp.concatenate([before, array, after], axis=dim)
    return array


def matern(targets, sources):
    squares = 0.0
    for component in range(targets.shape[-2]):
        offset_gap = targets[..., component, :, None] - sources[..., component, None, :]
        squares = squares + offset_gap * offset_gap
    scaled = ROOT_THREE * jnp.sqrt(squares) / LENGTH_SCALE
    return (1.0 + scaled) * jnp.exp(-scaled)


def per_device(
    points,
    charges,
    basis,
    transfer,
    skeleton,
    top_skeleton,
    near_mask,
    remote_dev,
    remote_leaf,
    far_mask,
    top_far,
):
    devices = lax.axis_size("leaf")
    device = lax.axis_index("leaf")
    local_count = points.shape[0]
    coords = points.shape[1]
    remote_slots = remote_dev.shape[1]
    near_reach = near_mask.shape[1] // 2
    far_reach = far_mask.shape[1] // 2
    node_count = top_skeleton.shape[0]
    capacity = min(local_count, (local_count * remote_slots + devices - 2) // (devices - 1) + 1)
    leaf_ids = jnp.arange(local_count, dtype=jnp.int32)
    leaf_pack = jnp.concatenate([points, charges], axis=1)
    widened = with_halo(leaf_pack, (("leaf", 0),), near_reach)
    weights = jnp.einsum("lnp,lpr->lnr", charges, basis, preferred_element_type=jnp.float32).astype(
        jnp.bfloat16
    )
    far_pack = jnp.concatenate([skeleton, weights], axis=1)
    far_wide = with_halo(far_pack, (("leaf", 0),), near_reach + far_reach)
    targets = ((device + 1 + remote_dev) % devices).reshape(-1)
    flat_leaf = remote_leaf.reshape(-1)
    onehot = (targets[:, None] == jnp.arange(devices, dtype=jnp.int32)[None, :]).astype(jnp.int32)
    before = jnp.cumsum(onehot, axis=0) - onehot
    position = jnp.sum(before * onehot, axis=1)
    points_wide = points.astype(jnp.float32)
    window_mask = jnp.concatenate(
        [
            near_mask[:, :near_reach].astype(jnp.bfloat16),
            jnp.ones((local_count, 1), jnp.bfloat16),
            near_mask[:, near_reach:].astype(jnp.bfloat16),
        ],
        axis=1,
    )
    wanted = (
        jnp.zeros((devices * capacity,), jnp.int32).at[targets * capacity + position].set(flat_leaf)
    )
    wanted = wanted.reshape(devices, capacity)
    fetched = lax.all_to_all(
        leaf_pack[lax.all_to_all(wanted, "leaf", split_axis=0, concat_axis=0, tiled=True)],
        "leaf",
        split_axis=0,
        concat_axis=0,
        tiled=True,
    )
    remote_pack = fetched[targets, position].reshape(
        local_count, remote_slots, leaf_pack.shape[1], leaf_pack.shape[2]
    )
    mask_all = jnp.concatenate(
        [window_mask, jnp.ones((local_count, remote_slots), jnp.bfloat16)], axis=1
    )

    def near_one(leaf_index):
        window = lax.dynamic_slice_in_dim(widened, leaf_index, 2 * near_reach + 1, 0)
        sources = jnp.concatenate([window, remote_pack[leaf_index]], axis=0)
        kernel = matern(points_wide[leaf_index], sources[:, :coords].astype(jnp.float32)).astype(
            jnp.bfloat16
        )
        kernel = kernel * mask_all[leaf_index][:, None, None]
        return jnp.einsum(
            "snq,spq->np", sources[:, coords:], kernel, preferred_element_type=jnp.float32
        )

    near_field = lax.map(near_one, leaf_ids)
    far_flags = far_mask.astype(jnp.bfloat16)

    def far_one(leaf_index):
        below = lax.dynamic_slice_in_dim(far_wide, leaf_index, far_reach, 0)
        above = lax.dynamic_slice_in_dim(
            far_wide, leaf_index + 2 * near_reach + far_reach + 1, far_reach, 0
        )
        sources = jnp.concatenate([below, above], axis=0)
        kernel = matern(
            skeleton[leaf_index].astype(jnp.float32), sources[:, :coords].astype(jnp.float32)
        ).astype(jnp.bfloat16)
        kernel = kernel * far_flags[leaf_index][:, None, None]
        return jnp.einsum(
            "snq,spq->np", sources[:, coords:], kernel, preferred_element_type=jnp.float32
        )

    far_terms = lax.map(far_one, leaf_ids)
    partial_weights = jnp.einsum(
        "lrs,lnr->ns", transfer, weights, preferred_element_type=jnp.float32
    )
    per_node = devices // node_count
    own_node = device // per_node
    empty_table = jnp.zeros((node_count,) + partial_weights.shape, jnp.float32)
    filled = lax.dynamic_update_slice(empty_table, partial_weights[None], (own_node, 0, 0))
    node_weights = lax.psum(filled, "leaf")
    far_nodes = top_far[own_node]
    node_kernel = matern(
        top_skeleton[own_node].astype(jnp.float32), top_skeleton[far_nodes].astype(jnp.float32)
    )
    expansion = jnp.einsum(
        "mrs,mns->nr", node_kernel, node_weights[far_nodes], precision=lax.Precision.HIGHEST
    ).astype(jnp.bfloat16)
    down = jnp.einsum("lrs,ns->lnr", transfer, expansion, preferred_element_type=jnp.float32)
    local_terms = (far_terms + down).astype(jnp.bfloat16)
    far_field = jnp.einsum("lpr,lnr->lnp", basis, local_terms, preferred_element_type=jnp.float32)
    return near_field + far_field


def solution(mesh):
    placed = (
        P(("parts", "leaf"), None, None),
        P(("parts", "leaf"), None, None),
        P(("parts", "leaf"), None, None),
        P(("parts", "leaf"), None, None),
        P(("parts", "leaf"), None, None),
        P("parts", None, None),
        P(("parts", "leaf"), None),
        P(("parts", "leaf"), None),
        P(("parts", "leaf"), None),
        P(("parts", "leaf"), None),
        P("parts", None),
    )
    return jax.shard_map(
        per_device,
        mesh=mesh,
        in_specs=placed,
        out_specs=P(("parts", "leaf"), None, None),
        check_vma=False,
    )
```

profile of v0, /device:TPU:1, one launch (start us, length us, event | category | flops | bytes accessed | tf_op | source)
XLA Modules:
  0.0 542.8 jit_solution(14808633145631308783)
XLA Ops:
  12.0 4.5 collective-permute-start.2
  16.5 1.9 collective-permute-start.3
  23.4 6.2 %all-to-all-start = ((s32[32,1,9]{2,1,0:T(1,128)}), s32[32,1,9]{2,1,0:T(1,128)S(1)}, u32[]{:S(2)}, u32[]{:S(2)}) async-start(s32[32,1,9]{2,1,0:T(1,128)} %bitcast.28), calls=%async_computation | async-start | bytes 32768 | tf_op jit(solution)/shard_map/all_to_all | solution.py:83
  32.9 3.5 collective-permute-start
  36.5 1.9 collective-permute-start.1
  45.7 14.2 %gather_fusion = bf16[288,40,256]{2,1,0:T(8,128)(2,1)} fusion(bf16[20,40,256]{2,1,0:T(8,128)(2,1)S(1)} %constant_dynamic-update-slice_fusion, s32[1024]{0:T(1024)S(1)} %pad_clamp_fusion.1), kind=kCustom, calls=%fused_computation | custom fusion | bytes 11797632 | tf_op jit(solution)/shard_map/gather | solution.py:83
  59.9 6.0 %all-to-all-start.1 = ((bf16[32,9,40,256]{3,2,1,0:T(8,128)(2,1)}), bf16[32,9,40,256]{3,2,1,0:T(8,128)(2,1)}, u32[]{:S(2)}, u32[]{:S(2)}) async-start(bf16[32,9,40,256]{3,2,1,0:T(8,128)(2,1)} %bitcast.199), calls=%async_computation.1 | async-start | bytes 11796480 | tf_op jit(solution)/shard_map/all_to_all | solution.py:82
  66.1 120.3 %while.25 = (s32[]{:T(128)}, f32[20,32,128]{2,1,0:T(8,128)S(1)}, s32[20]{0:T(128)S(1)}, bf16[40,40,128]{2,1,0:T(8,128)(2,1)S(1)}, bf16[20,8,128]{2,1,0:T(8,128)(...) while((s32[]{:T(128)}, f32[20,32,128]{2,1,0:T(8,128)S(1)}, ...), condition=%wide.region_7.8_spmd, body=%wide.region_6.7_spmd.sunk | while | flops 9192459 | bytes 437014 | solution.py:124
  191.8 6.8 %all-to-all-done.1 = bf16[32,9,40,256]{3,2,1,0:T(8,128)(2,1)} async-done(((bf16[32,9,40,256]{3,2,1,0:T(8,128)(2,1)}), bf16[32,9,40,256]{3,2,1,0:T(8,128)(2,1)}, u32[]{:S(2)}, u32[]{:S(2)}) %all-to-all-start.1) | async-done | bytes 5898272 | tf_op jit(solution)/shard_map/all_to_all | solution.py:82
  198.5 6.8 %gather_fusion.1 = bf16[240,40,256]{2,1,0:T(8,128)(2,1)} fusion(bf16[32,9,40,256]{3,2,1,0:T(8,128)(2,1)} %all-to-all-done.1, s32[240]{0:T(256)S(1)} %bitcast.200), kind=kCustom, calls=%fused_computation.1 | custom fusion | bytes 9832320 | tf_op jit(solution)/shard_map/gather | solution.py:89
  205.3 328.7 %while.24 = (s32[]{:T(128)}, f32[20,32,256]{2,1,0:T(8,128)}, s32[20]{0:T(128)S(1)}, bf16[34,40,256]{2,1,0:T(8,128)(2,1)S(1)}, bf16[20,12,40,256]{3,2,1,0:T(8,128...) while((s32[]{:T(128)}, f32[20,32,256]{2,1,0:T(8,128)}, ...), condition=%wide.region_5.6_spmd, body=%wide.region_4.5_spmd.sunk | while | flops 165003280 | bytes 3597326 | solution.py:107
  212.3 9.5 %fusion.142 = f32[20,32,256]{2,1,0:T(8,128)} fusion(f32[20,32,256]{2,1,0:T(8,128)} %get-tuple-element.469, s32[]{:T(128)} %get-tuple-element.468, f32[27,256]{1,0:T(8,128)S(1)} %get-tuple-element.396, f32[256]{0:T(256)S(1)} %bitcast.210, f32[27,256]{1,0:T(8,128)S(1)} %get-tuple-element.398, f32[256]{0:T(256)S(1)} %bitcast.204, ...), kind=kOutput, calls=%fused_computation.10.clone.1 | convolution fusion | flops 164782080 | bytes 815670 | tf_op jit(solution)/shard_map/while/body/eval_jaxpr/snq,spq->np/dot_general | solution.py:103
  228.7 9.5 %fusion.142 = f32[20,32,256]{2,1,0:T(8,128)} fusion(f32[20,32,256]{2,1,0:T(8,128)} %get-tuple-element.469, s32[]{:T(128)} %get-tuple-element.468, f32[27,256]{1,0:T(8,128)S(1)} %get-tuple-element.396, f32[256]{0:T(256)S(1)} %bitcast.210, f32[27,256]{1,0:T(8,128)S(1)} %get-tuple-element.398, f32[256]{0:T(256)S(1)} %bitcast.204, ...), kind=kOutput, calls=%fused_computation.10.clone.1 | convolution fusion | flops 164782080 | bytes 815670 | tf_op jit(solution)/shard_map/while/body/eval_jaxpr/snq,spq->np/dot_general | solution.py:103
  245.2 9.5 %fusion.142 = f32[20,32,256]{2,1,0:T(8,128)} fusion(f32[20,32,256]{2,1,0:T(8,128)} %get-tuple-element.469, s32[]{:T(128)} %get-tuple-element.468, f32[27,256]{1,0:T(8,128)S(1)} %get-tuple-element.396, f32[256]{0:T(256)S(1)} %bitcast.210, f32[27,256]{1,0:T(8,128)S(1)} %get-tuple-element.398, f32[256]{0:T(256)S(1)} %bitcast.204, ...), kind=kOutput, calls=%fused_computation.10.clone.1 | convolution fusion | flops 164782080 | bytes 815670 | tf_op jit(solution)/shard_map/while/body/eval_jaxpr/snq,spq->np/dot_general | solution.py:103
  261.6 9.5 %fusion.142 = f32[20,32,256]{2,1,0:T(8,128)} fusion(f32[20,32,256]{2,1,0:T(8,128)} %get-tuple-element.469, s32[]{:T(128)} %get-tuple-element.468, f32[27,256]{1,0:T(8,128)S(1)} %get-tuple-element.396, f32[256]{0:T(256)S(1)} %bitcast.210, f32[27,256]{1,0:T(8,128)S(1)} %get-tuple-element.398, f32[256]{0:T(256)S(1)} %bitcast.204, ...), kind=kOutput, calls=%fused_computation.10.clone.1 | convolution fusion | flops 164782080 | bytes 815670 | tf_op jit(solution)/shard_map/while/body/eval_jaxpr/snq,spq->np/dot_general | solution.py:103
  278.1 9.5 %fusion.142 = f32[20,32,256]{2,1,0:T(8,128)} fusion(f32[20,32,256]{2,1,0:T(8,128)} %get-tuple-element.469, s32[]{:T(128)} %get-tuple-element.468, f32[27,256]{1,0:T(8,128)S(1)} %get-tuple-element.396, f32[256]{0:T(256)S(1)} %bitcast.210, f32[27,256]{1,0:T(8,128)S(1)} %get-tuple-element.398, f32[256]{0:T(256)S(1)} %bitcast.204, ...), kind=kOutput, calls=%fused_computation.10.clone.1 | convolution fusion | flops 164782080 | bytes 815670 | tf_op jit(solution)/shard_map/while/body/eval_jaxpr/snq,spq->np/dot_general | solution.py:103
  294.6 9.5 %fusion.142 = f32[20,32,256]{2,1,0:T(8,128)} fusion(f32[20,32,256]{2,1,0:T(8,128)} %get-tuple-element.469, s32[]{:T(128)} %get-tuple-element.468, f32[27,256]{1,0:T(8,128)S(1)} %get-tuple-element.396, f32[256]{0:T(256)S(1)} %bitcast.210, f32[27,256]{1,0:T(8,128)S(1)} %get-tuple-element.398, f32[256]{0:T(256)S(1)} %bitcast.204, ...), kind=kOutput, calls=%fused_computation.10.clone.1 | convolution fusion | flops 164782080 | bytes 815670 | tf_op jit(solution)/shard_map/while/body/eval_jaxpr/snq,spq->np/dot_general | solution.py:103
  311.0 9.5 %fusion.142 = f32[20,32,256]{2,1,0:T(8,128)} fusion(f32[20,32,256]{2,1,0:T(8,128)} %get-tuple-element.469, s32[]{:T(128)} %get-tuple-element.468, f32[27,256]{1,0:T(8,128)S(1)} %get-tuple-element.396, f32[256]{0:T(256)S(1)} %bitcast.210, f32[27,256]{1,0:T(8,128)S(1)} %get-tuple-element.398, f32[256]{0:T(256)S(1)} %bitcast.204, ...), kind=kOutput, calls=%fused_computation.10.clone.1 | convolution fusion | flops 164782080 | bytes 815670 | tf_op jit(solution)/shard_map/while/body/eval_jaxpr/snq,spq->np/dot_general | solution.py:103
  327.5 9.5 %fusion.142 = f32[20,32,256]{2,1,0:T(8,128)} fusion(f32[20,32,256]{2,1,0:T(8,128)} %get-tuple-element.469, s32[]{:T(128)} %get-tuple-element.468, f32[27,256]{1,0:T(8,128)S(1)} %get-tuple-element.396, f32[256]{0:T(256)S(1)} %bitcast.210, f32[27,256]{1,0:T(8,128)S(1)} %get-tuple-element.398, f32[256]{0:T(256)S(1)} %bitcast.204, ...), kind=kOutput, calls=%fused_computation.10.clone.1 | convolution fusion | flops 164782080 | bytes 815670 | tf_op jit(solution)/shard_map/while/body/eval_jaxpr/snq,spq->np/dot_general | solution.py:103
  343.9 9.5 %fusion.142 = f32[20,32,256]{2,1,0:T(8,128)} fusion(f32[20,32,256]{2,1,0:T(8,128)} %get-tuple-element.469, s32[]{:T(128)} %get-tuple-element.468, f32[27,256]{1,0:T(8,128)S(1)} %get-tuple-element.396, f32[256]{0:T(256)S(1)} %bitcast.210, f32[27,256]{1,0:T(8,128)S(1)} %get-tuple-element.398, f32[256]{0:T(256)S(1)} %bitcast.204, ...), kind=kOutput, calls=%fused_computation.10.clone.1 | convolution fusion | flops 164782080 | bytes 815670 | tf_op jit(solution)/shard_map/while/body/eval_jaxpr/snq,spq->np/dot_general | solution.py:103
  360.3 9.5 %fusion.142 = f32[20,32,256]{2,1,0:T(8,128)} fusion(f32[20,32,256]{2,1,0:T(8,128)} %get-tuple-element.469, s32[]{:T(128)} %get-tuple-element.468, f32[27,256]{1,0:T(8,128)S(1)} %get-tuple-element.396, f32[256]{0:T(256)S(1)} %bitcast.210, f32[27,256]{1,0:T(8,128)S(1)} %get-tuple-element.398, f32[256]{0:T(256)S(1)} %bitcast.204, ...), kind=kOutput, calls=%fused_computation.10.clone.1 | convolution fusion | flops 164782080 | bytes 815670 | tf_op jit(solution)/shard_map/while/body/eval_jaxpr/snq,spq->np/dot_general | solution.py:103
  376.7 9.5 %fusion.142 = f32[20,32,256]{2,1,0:T(8,128)} fusion(f32[20,32,256]{2,1,0:T(8,128)} %get-tuple-element.469, s32[]{:T(128)} %get-tuple-element.468, f32[27,256]{1,0:T(8,128)S(1)} %get-tuple-element.396, f32[256]{0:T(256)S(1)} %bitcast.210, f32[27,256]{1,0:T(8,128)S(1)} %get-tuple-element.398, f32[256]{0:T(256)S(1)} %bitcast.204, ...), kind=kOutput, calls=%fused_computation.10.clone.1 | convolution fusion | flops 164782080 | bytes 815670 | tf_op jit(solution)/shard_map/while/body/eval_jaxpr/snq,spq->np/dot_general | solution.py:103
  393.1 9.5 %fusion.142 = f32[20,32,256]{2,1,0:T(8,128)} fusion(f32[20,32,256]{2,1,0:T(8,128)} %get-tuple-element.469, s32[]{:T(128)} %get-tuple-element.468, f32[27,256]{1,0:T(8,128)S(1)} %get-tuple-element.396, f32[256]{0:T(256)S(1)} %bitcast.210, f32[27,256]{1,0:T(8,128)S(1)} %get-tuple-element.398, f32[256]{0:T(256)S(1)} %bitcast.204, ...), kind=kOutput, calls=%fused_computation.10.clone.1 | convolution fusion | flops 164782080 | bytes 815670 | tf_op jit(solution)/shard_map/while/body/eval_jaxpr/snq,spq->np/dot_general | solution.py:103
  409.5 9.5 %fusion.142 = f32[20,32,256]{2,1,0:T(8,128)} fusion(f32[20,32,256]{2,1,0:T(8,128)} %get-tuple-element.469, s32[]{:T(128)} %get-tuple-element.468, f32[27,256]{1,0:T(8,128)S(1)} %get-tuple-element.396, f32[256]{0:T(256)S(1)} %bitcast.210, f32[27,256]{1,0:T(8,128)S(1)} %get-tuple-element.398, f32[256]{0:T(256)S(1)} %bitcast.204, ...), kind=kOutput, calls=%fused_computation.10.clone.1 | convolution fusion | flops 164782080 | bytes 815670 | tf_op jit(solution)/shard_map/while/body/eval_jaxpr/snq,spq->np/dot_general | solution.py:103
  425.9 9.5 %fusion.142 = f32[20,32,256]{2,1,0:T(8,128)} fusion(f32[20,32,256]{2,1,0:T(8,128)} %get-tuple-element.469, s32[]{:T(128)} %get-tuple-element.468, f32[27,256]{1,0:T(8,128)S(1)} %get-tuple-element.396, f32[256]{0:T(256)S(1)} %bitcast.210, f32[27,256]{1,0:T(8,128)S(1)} %get-tuple-element.398, f32[256]{0:T(256)S(1)} %bitcast.204, ...), kind=kOutput, calls=%fused_computation.10.clone.1 | convolution fusion | flops 164782080 | bytes 815670 | tf_op jit(solution)/shard_map/while/body/eval_jaxpr/snq,spq->np/dot_general | solution.py:103
  442.3 9.5 %fusion.142 = f32[20,32,256]{2,1,0:T(8,128)} fusion(f32[20,32,256]{2,1,0:T(8,128)} %get-tuple-element.469, s32[]{:T(128)} %get-tuple-element.468, f32[27,256]{1,0:T(8,128)S(1)} %get-tuple-element.396, f32[256]{0:T(256)S(1)} %bitcast.210, f32[27,256]{1,0:T(8,128)S(1)} %get-tuple-element.398, f32[256]{0:T(256)S(1)} %bitcast.204, ...), kind=kOutput, calls=%fused_computation.10.clone.1 | convolution fusion | flops 164782080 | bytes 815670 | tf_op jit(solution)/shard_map/while/body/eval_jaxpr/snq,spq->np/dot_general | solution.py:103
  458.7 9.5 %fusion.142 = f32[20,32,256]{2,1,0:T(8,128)} fusion(f32[20,32,256]{2,1,0:T(8,128)} %get-tuple-element.469, s32[]{:T(128)} %get-tuple-element.468, f32[27,256]{1,0:T(8,128)S(1)} %get-tuple-element.396, f32[256]{0:T(256)S(1)} %bitcast.210, f32[27,256]{1,0:T(8,128)S(1)} %get-tuple-element.398, f32[256]{0:T(256)S(1)} %bitcast.204, ...), kind=kOutput, calls=%fused_computation.10.clone.1 | convolution fusion | flops 164782080 | bytes 815670 | tf_op jit(solution)/shard_map/while/body/eval_jaxpr/snq,spq->np/dot_general | solution.py:103
  475.1 9.5 %fusion.142 = f32[20,32,256]{2,1,0:T(8,128)} fusion(f32[20,32,256]{2,1,0:T(8,128)} %get-tuple-element.469, s32[]{:T(128)} %get-tuple-element.468, f32[27,256]{1,0:T(8,128)S(1)} %get-tuple-element.396, f32[256]{0:T(256)S(1)} %bitcast.210, f32[27,256]{1,0:T(8,128)S(1)} %get-tuple-element.398, f32[256]{0:T(256)S(1)} %bitcast.204, ...), kind=kOutput, calls=%fused_computation.10.clone.1 | convolution fusion | flops 164782080 | bytes 815670 | tf_op jit(solution)/shard_map/while/body/eval_jaxpr/snq,spq->np/dot_general | solution.py:103
  491.6 9.5 %fusion.142 = f32[20,32,256]{2,1,0:T(8,128)} fusion(f32[20,32,256]{2,1,0:T(8,128)} %get-tuple-element.469, s32[]{:T(128)} %get-tuple-element.468, f32[27,256]{1,0:T(8,128)S(1)} %get-tuple-element.396, f32[256]{0:T(256)S(1)} %bitcast.210, f32[27,256]{1,0:T(8,128)S(1)} %get-tuple-element.398, f32[256]{0:T(256)S(1)} %bitcast.204, ...), kind=kOutput, calls=%fused_computation.10.clone.1 | convolution fusion | flops 164782080 | bytes 815670 | tf_op jit(solution)/shard_map/while/body/eval_jaxpr/snq,spq->np/dot_general | solution.py:103
  508.0 9.5 %fusion.142 = f32[20,32,256]{2,1,0:T(8,128)} fusion(f32[20,32,256]{2,1,0:T(8,128)} %get-tuple-element.469, s32[]{:T(128)} %get-tuple-element.468, f32[27,256]{1,0:T(8,128)S(1)} %get-tuple-element.396, f32[256]{0:T(256)S(1)} %bitcast.210, f32[27,256]{1,0:T(8,128)S(1)} %get-tuple-element.398, f32[256]{0:T(256)S(1)} %bitcast.204, ...), kind=kOutput, calls=%fused_computation.10.clone.1 | convolution fusion | flops 164782080 | bytes 815670 | tf_op jit(solution)/shard_map/while/body/eval_jaxpr/snq,spq->np/dot_general | solution.py:103
  524.5 9.5 %fusion.142 = f32[20,32,256]{2,1,0:T(8,128)} fusion(f32[20,32,256]{2,1,0:T(8,128)} %get-tuple-element.469, s32[]{:T(128)} %get-tuple-element.468, f32[27,256]{1,0:T(8,128)S(1)} %get-tuple-element.396, f32[256]{0:T(256)S(1)} %bitcast.210, f32[27,256]{1,0:T(8,128)S(1)} %get-tuple-element.398, f32[256]{0:T(256)S(1)} %bitcast.204, ...), kind=kOutput, calls=%fused_computation.10.clone.1 | convolution fusion | flops 164782080 | bytes 815670 | tf_op jit(solution)/shard_map/while/body/eval_jaxpr/snq,spq->np/dot_general | solution.py:103
  534.0 2.0 add.320
  (544 shorter events, 136.9 us)
Async XLA Ops:
  6.5 1.3 copy-start
  6.5 179.8 %all-reduce.3.cloned.1.call-start = ((), (), s32[]{:S(2)}) async-start(), calls=%async_computation.2 | async-start | bytes 524288 | tf_op jit(solution)/shard_map/psum | solution.py:132
  10.5 0.7 copy-start.2
  12.0 53.9 %collective-permute-start.2 = (bf16[10,40,128]{2,1,0:T(8,128)(2,1)S(1)}, bf16[10,40,128]{2,1,0:T(8,128)(2,1)S(1)}, u32[]{:S(2)}, u32[]{:S(2)}) collective-permute-start(bf16[10,40,128]{2,1,0:T(8,128)(2,1)S(1)} %get-tuple-element.246), channel_id=1, source_target_pairs={{0,1},{1,2},{2,3},{3,4},{4,5},{5,6},{6,7},{7,8},{8,9},{9,10},{10,1... | collective-permute-start | bytes 307208 | tf_op jit(solution)/shard_map/ppermute | solution.py:19
  16.5 49.4 %collective-permute-start.3 = (bf16[10,40,128]{2,1,0:T(8,128)(2,1)S(1)}, bf16[10,40,128]{2,1,0:T(8,128)(2,1)S(1)}, u32[]{:S(2)}, u32[]{:S(2)}) collective-permute-start(bf16[10,40,128]{2,1,0:T(8,128)(2,1)S(1)} %get-tuple-element.247), channel_id=1, source_target_pairs={{1,0},{2,1},{3,2},{4,3},{5,4},{6,5},{7,6},{8,7},{9,8},{10,9},{11,1... | collective-permute-start | bytes 307208 | tf_op jit(solution)/shard_map/ppermute | solution.py:20
  23.4 22.2 %all-to-all-start = ((s32[32,1,9]{2,1,0:T(1,128)}), s32[32,1,9]{2,1,0:T(1,128)S(1)}, u32[]{:S(2)}, u32[]{:S(2)}) async-start(s32[32,1,9]{2,1,0:T(1,128)} %bitcast.28), calls=%async_computation | async-start | bytes 32768 | tf_op jit(solution)/shard_map/all_to_all | solution.py:83
  32.9 157.7 %collective-permute-start = (bf16[7,40,256]{2,1,0:T(8,128)(2,1)}, bf16[7,40,256]{2,1,0:T(8,128)(2,1)}, u32[]{:S(2)}, u32[]{:S(2)}) collective-permute-start(bf16[7,40,256]{2,1,0:T(8,128)(2,1)} %get-tuple-element.244), channel_id=1, source_target_pairs={{0,1},{1,2},{2,3},{3,4},{4,5},{5,6},{6,7},{7,8},{8,9},{9,10},{10,1... | collective-permute-start | bytes 430088 | tf_op jit(solution)/shard_map/ppermute | solution.py:19
  36.5 154.2 %collective-permute-start.1 = (bf16[7,40,256]{2,1,0:T(8,128)(2,1)S(1)}, bf16[7,40,256]{2,1,0:T(8,128)(2,1)}, u32[]{:S(2)}, u32[]{:S(2)}) collective-permute-start(bf16[7,40,256]{2,1,0:T(8,128)(2,1)S(1)} %get-tuple-element.245), channel_id=1, source_target_pairs={{1,0},{2,1},{3,2},{4,3},{5,4},{6,5},{7,6},{8,7},{9,8},{10,9},{11,1... | collective-permute-start | bytes 430088 | tf_op jit(solution)/shard_map/ppermute | solution.py:20
  59.9 6.1 %copy-start.3 = (bf16[20,8,128]{2,1,0:T(8,128)(2,1)S(1)}, bf16[20,8,128]{2,1,0:T(8,128)(2,1)}, u32[]{:S(2)}) copy-start(bf16[20,8,128]{2,1,0:T(8,128)(2,1)} %param.19) | copy-start | bytes 122884
  59.9 138.6 %all-to-all-start.1 = ((bf16[32,9,40,256]{3,2,1,0:T(8,128)(2,1)}), bf16[32,9,40,256]{3,2,1,0:T(8,128)(2,1)}, u32[]{:S(2)}, u32[]{:S(2)}) async-start(bf16[32,9,40,256]{3,2,1,0:T(8,128)(2,1)} %bitcast.199), calls=%async_computation.1 | async-start | bytes 11796480 | tf_op jit(solution)/shard_map/all_to_all | solution.py:82
  66.0 122.0 %copy-start.4 = (f32[8,1,128]{2,1,0:T(1,128)S(1)}, f32[8,1,128]{2,1,0:T(1,128)}, u32[]{:S(2)}) copy-start(f32[8,1,128]{2,1,0:T(1,128)} %get-tuple-element.251) | copy-start | bytes 12292
  66.0 122.0 %copy-start.5 = (f32[8,1,128]{2,1,0:T(1,128)S(1)}, f32[8,1,128]{2,1,0:T(1,128)}, u32[]{:S(2)}) copy-start(f32[8,1,128]{2,1,0:T(1,128)} %get-tuple-element.252) | copy-start | bytes 12292
  66.0 122.0 %copy-start.6 = (f32[8,1,128]{2,1,0:T(1,128)S(1)}, f32[8,1,128]{2,1,0:T(1,128)}, u32[]{:S(2)}) copy-start(f32[8,1,128]{2,1,0:T(1,128)} %get-tuple-element.253) | copy-start | bytes 12292
  66.0 122.0 %copy-start.7 = (f32[8,1,128]{2,1,0:T(1,128)S(1)}, f32[8,1,128]{2,1,0:T(1,128)}, u32[]{:S(2)}) copy-start(f32[8,1,128]{2,1,0:T(1,128)} %get-tuple-element.254) | copy-start | bytes 12292
  66.0 122.0 %copy-start.8 = (f32[8,1,128]{2,1,0:T(1,128)S(1)}, f32[8,1,128]{2,1,0:T(1,128)}, u32[]{:S(2)}) copy-start(f32[8,1,128]{2,1,0:T(1,128)} %get-tuple-element.255) | copy-start | bytes 12292
  66.0 122.0 %copy-start.9 = (f32[8,1,128]{2,1,0:T(1,128)S(1)}, f32[8,1,128]{2,1,0:T(1,128)}, u32[]{:S(2)}) copy-start(f32[8,1,128]{2,1,0:T(1,128)} %get-tuple-element.256) | copy-start | bytes 12292
  66.1 122.0 %copy-start.10 = (f32[8,1,128]{2,1,0:T(1,128)S(1)}, f32[8,1,128]{2,1,0:T(1,128)}, u32[]{:S(2)}) copy-start(f32[8,1,128]{2,1,0:T(1,128)} %get-tuple-element.257) | copy-start | bytes 12292
  66.1 122.0 %copy-start.11 = (f32[128]{0:T(128)S(1)}, f32[128]{0:T(128)}, u32[]{:S(2)}) copy-start(f32[128]{0:T(128)} %get-tuple-element.260) | copy-start | bytes 1540
  66.1 123.8 %copy-start.1 = (bf16[20,128,128]{2,1,0:T(8,128)(2,1)S(1)}, bf16[20,128,128]{2,1,0:T(8,128)(2,1)}, u32[]{:S(2)}) copy-start(bf16[20,128,128]{2,1,0:T(8,128)(2,1)} %param.18) | copy-start | bytes 1966084
Sparse Core Ops, SparseCore 0:
  12.9 162.8 all-reduce.2
where the time goes:
time: 549 us; the launch traced here: 543 us
  matrix products  207 us (38%)
  loops' own time  149 us (27%)
  local copies, waits for them, and re-layouts  132 us (24%)
  starting transfers between devices  24.1 us (4%)
  between operations  13.8 us (3%)
  other arithmetic  9.68 us (2%)
  waiting for transfers between devices  6.79 us (1%)
    dot_general x20, matrix products, near_one(): jnp.einsum('snq,spq->np', sources[:, coords:], kernel, preferred_element_...  190 us
    another operation x1, loops' own time, per_device(): far_terms = lax.map(far_one, leaf_ids)  80.2 us
    another operation x1, loops' own time, per_device(): near_field = lax.map(near_one, leaf_ids)  68.6 us
    dynamic_slice x40, local copies, waits for them, and re-layouts, per_device(): near_field = lax.map(near_one, leaf_ids)  25.6 us
    slice x20, local copies, waits for them, and re-layouts, matern(): targets[..., component, :, None] - sources[..., component, None, :]  20.3 us
    squeeze x20, local copies, waits for them, and re-layouts, near_one(): sources = jnp.concatenate([window, remote_pack[leaf_index]], axis=0)  19.3 us
    gather x1, local copies, waits for them, and re-layouts, per_device(): leaf_pack[lax.all_to_all(wanted, 'leaf', split_axis=0, concat_axis=0, til...  14.2 us
    mul x20, local copies, waits for them, and re-layouts, far_one(): kernel = kernel * far_flags[leaf_index][:, None, None]  13.4 us
  transfers between devices with their start and end apart: 7, of which 1 were waited for; matrix products, arithmetic and copies ran while one was open for 14% of the time, Pallas kernels for 0%

commit v1 on v0

v1 whole, which is shorter than its diff:
```python
import functools
import math

import jax
import jax.numpy as jnp
from jax import lax
from jax.experimental import pallas as pl
from jax.experimental.pallas import tpu as pltpu
from jax.sharding import PartitionSpec as P

ROOT_THREE = math.sqrt(3.0)
LENGTH_SCALE = 1.0
ALPHA = 3.0 / (LENGTH_SCALE * LENGTH_SCALE)
UNROLL = 8
VMEM_LIMIT = 56 * 2**20


def with_halo(array, sides, width):
    for axis, dim in sides:
        count, length = (lax.axis_size(axis), array.shape[dim])
        up = [(i, (i + 1) % count) for i in range(count - 1)]
        down = [(j, i) for i, j in up]
        last = lax.slice_in_dim(array, length - width, length, axis=dim)
        initial = lax.slice_in_dim(array, 0, width, axis=dim)
        before = lax.ppermute(last, axis, up)
        after = lax.ppermute(initial, axis, down)
        array = jnp.concatenate([before, array, after], axis=dim)
    return array


def matern(targets, sources):
    squares = 0.0
    for component in range(targets.shape[-2]):
        offset_gap = targets[..., component, :, None] - sources[..., component, None, :]
        squares = squares + offset_gap * offset_gap
    scaled = ROOT_THREE * jnp.sqrt(squares) / LENGTH_SCALE
    return (1.0 + scaled) * jnp.exp(-scaled)


def reduced(value):
    return lax.reduce_precision(value, 8, 7)


def rounded(value):
    return value.astype(jnp.bfloat16).astype(jnp.float32)


def three_parts(value, narrow):
    high = narrow(value)
    middle = narrow(value - high)
    return high, middle, narrow(value - high - middle)


def target_side(points):
    wide = points.astype(jnp.float32)
    cross = three_parts(-2.0 * ALPHA * wide, reduced)
    norms = three_parts(ALPHA * jnp.sum(wide * wide, axis=1, keepdims=True), reduced)
    one = jnp.ones_like(norms[0])
    zero = jnp.zeros_like(one)
    rows = jnp.concatenate([*cross, *norms, one, one, one, zero, zero], axis=1)
    return jnp.swapaxes(rows.astype(jnp.bfloat16), 1, 2)


def source_side(points):
    high, middle, low = three_parts(
        ALPHA * jnp.sum(points * points, axis=0, keepdims=True), rounded
    )
    row = lax.broadcasted_iota(jnp.int32, points.shape, 0)
    tail = jnp.where(
        row < 3,
        1.0,
        jnp.where(row == 3, high, jnp.where(row == 4, middle, jnp.where(row == 5, low, 0.0))),
    )
    return jnp.concatenate([points, points, points, tail], axis=0).astype(jnp.bfloat16)


def kernel_values(squares):
    squares = jnp.maximum(squares, 1e-20)
    scaled = squares * lax.rsqrt(squares)
    return ((1.0 + scaled) * jnp.exp(-scaled)).astype(jnp.bfloat16)


def dot_last(a, b):
    return lax.dot_general(a, b, (((1,), (1,)), ((), ())), preferred_element_type=jnp.float32)


def pair_kernel(rhs, has_base, count_ref, source_ref, target_ref, scale_ref, side_ref, pack_ref, *rest):
    out_ref = rest[-1]
    out_ref[...] = rest[0][...] if has_base else jnp.zeros_like(out_ref)

    def step(number, carry):
        pairs = []
        for slot in range(UNROLL):
            entry = number * UNROLL + slot
            block = pack_ref[source_ref[entry]]
            squares = jnp.dot(
                side_ref[target_ref[entry]],
                source_side(block[rhs:].astype(jnp.float32)),
                preferred_element_type=jnp.float32,
            )
            pairs.append((entry, block, squares))
        sums = []
        for entry, block, squares in pairs:
            charges = block[:rhs] * scale_ref[entry].astype(jnp.bfloat16)
            sums.append((target_ref[entry], dot_last(charges, kernel_values(squares))))
        for target, term in sums:
            out_ref[target] += term
        return carry

    lax.fori_loop(0, (count_ref[0] + UNROLL - 1) // UNROLL, step, 0)


def sum_pairs(pairs, side, pack, base=None, name="pairs"):
    leaves, length = side.shape[:2]
    rhs = pack.shape[1] - 8
    scalars = pl.BlockSpec(memory_space=pltpu.SMEM)
    vectors = pl.BlockSpec(memory_space=pltpu.VMEM)
    extra = [] if base is None else [base]
    work = pairs[1].shape[0] * length * pack.shape[2]
    return pl.pallas_call(
        functools.partial(pair_kernel, rhs, base is not None),
        out_shape=jax.ShapeDtypeStruct((leaves, rhs, length), jnp.float32),
        in_specs=[scalars] * 4 + [vectors] * (2 + len(extra)),
        out_specs=vectors,
        compiler_params=pltpu.CompilerParams(vmem_limit_bytes=VMEM_LIMIT),
        cost_estimate=pl.CostEstimate(
            flops=2 * work * 64, bytes_accessed=2 * pack.size, transcendentals=2 * work
        ),
        name=name,
    )(*pairs, side, pack, *extra)


def far_kernel(rhs, near, far, mask_ref, side_ref, pack_ref, transfer_ref, expansion_ref, basis_ref, base_ref, out_ref):
    def one(leaf, carry):
        local = dot_last(expansion_ref[...], transfer_ref[leaf])
        for slot in range(2 * far):
            offset = slot if slot < far else slot + 2 * near + 1
            block = pack_ref[leaf + offset]
            squares = jnp.dot(
                side_ref[leaf],
                source_side(block[rhs:].astype(jnp.float32)),
                preferred_element_type=jnp.float32,
            )
            flag = mask_ref[leaf, slot].astype(jnp.float32).astype(jnp.bfloat16)
            local = local + dot_last(block[:rhs] * flag, kernel_values(squares))
        out_ref[leaf] = base_ref[leaf] + dot_last(local.astype(jnp.bfloat16), basis_ref[leaf])
        return carry

    lax.fori_loop(0, out_ref.shape[0], one, 0)


def listed(keep, source, target):
    keep, source, target = keep.reshape(-1), source.reshape(-1), target.reshape(-1)
    total = keep.shape[0]
    room = -(-total // UNROLL) * UNROLL
    ids = jnp.arange(total, dtype=jnp.int32)
    place = jnp.sum(jnp.where((ids[None, :] < ids[:, None]) & keep[None, :], 1, 0), axis=1)
    slots = jnp.arange(room, dtype=jnp.int32)
    hit = (place[None, :] == slots[:, None]) & keep[None, :]
    sources = jnp.sum(jnp.where(hit, source[None, :], 0), axis=1)
    targets = jnp.sum(jnp.where(hit, target[None, :], 0), axis=1)
    count = jnp.sum(keep.astype(jnp.int32))
    scales = (slots < count).astype(jnp.float32)
    return count.reshape(1), sources.astype(jnp.int32), targets.astype(jnp.int32), scales


def per_device(
    points,
    charges,
    basis,
    transfer,
    skeleton,
    top_skeleton,
    near_mask,
    remote_dev,
    remote_leaf,
    far_mask,
    top_far,
):
    devices = lax.axis_size("leaf")
    device = lax.axis_index("leaf")
    local_count, rhs = charges.shape[:2]
    near_reach = near_mask.shape[1] // 2
    far_reach = far_mask.shape[1] // 2
    node_count = top_skeleton.shape[0]
    leaf_pack = jnp.concatenate([charges, points], axis=1)
    gathered = lax.all_gather(leaf_pack, "leaf", axis=0, tiled=True)

    weights = jnp.einsum("lnp,lpr->lnr", charges, basis, preferred_element_type=jnp.float32).astype(
        jnp.bfloat16
    )
    far_pack = jnp.concatenate([weights, skeleton], axis=1)
    far_wide = with_halo(far_pack, (("leaf", 0),), near_reach + far_reach)
    partial_weights = jnp.einsum(
        "lrs,lnr->ns", transfer, weights, preferred_element_type=jnp.float32
    )
    per_node = devices // node_count
    own_node = device // per_node
    node_weights = lax.all_gather(partial_weights, "leaf", axis=0)
    node_weights = node_weights.reshape((node_count, per_node) + partial_weights.shape).sum(axis=1)
    far_nodes = top_far[own_node]
    node_kernel = matern(
        top_skeleton[own_node].astype(jnp.float32), top_skeleton[far_nodes].astype(jnp.float32)
    )
    expansion = jnp.einsum(
        "mrs,mns->nr", node_kernel, node_weights[far_nodes], precision=lax.Precision.HIGHEST
    ).astype(jnp.bfloat16)

    leaf_ids = jnp.arange(local_count, dtype=jnp.int32)
    reach = jnp.arange(-near_reach, near_reach + 1, dtype=jnp.int32)
    window = leaf_ids[:, None] + reach[None, :]
    inside = (window >= 0) & (window < local_count)
    wanted = jnp.concatenate(
        [near_mask[:, :near_reach], jnp.ones((local_count, 1), jnp.int32), near_mask[:, near_reach:]],
        axis=1,
    ) != 0
    window_targets = jnp.broadcast_to(leaf_ids[:, None], window.shape)
    own_pairs = listed(wanted & inside, window, window_targets)
    distant = window + device * local_count
    crossing = wanted & ~inside & (distant >= 0) & (distant < devices * local_count)
    remote = (device + 1 + remote_dev) % devices * local_count + remote_leaf
    other_pairs = listed(
        jnp.concatenate([crossing, jnp.ones(remote.shape, bool)], axis=1),
        jnp.concatenate([distant, remote], axis=1),
        jnp.broadcast_to(leaf_ids[:, None], (local_count, window.shape[1] + remote.shape[1])),
    )

    side = target_side(points)
    own_field = sum_pairs(own_pairs, side, leaf_pack, name="own_pairs")
    scalars = pl.BlockSpec(memory_space=pltpu.SMEM)
    vectors = pl.BlockSpec(memory_space=pltpu.VMEM)
    with_far = pl.pallas_call(
        functools.partial(far_kernel, rhs, near_reach, far_reach),
        out_shape=jax.ShapeDtypeStruct(own_field.shape, jnp.float32),
        in_specs=[scalars] + [vectors] * 6,
        out_specs=vectors,
        compiler_params=pltpu.CompilerParams(vmem_limit_bytes=VMEM_LIMIT),
        name="far_field",
    )(far_mask, target_side(skeleton), far_wide, transfer, expansion, basis, own_field)
    return sum_pairs(other_pairs, side, gathered, with_far, name="other_pairs")


def solution(mesh):
    placed = (
        P(("parts", "leaf"), None, None),
        P(("parts", "leaf"), None, None),
        P(("parts", "leaf"), None, None),
        P(("parts", "leaf"), None, None),
        P(("parts", "leaf"), None, None),
        P("parts", None, None),
        P(("parts", "leaf"), None),
        P(("parts", "leaf"), None),
        P(("parts", "leaf"), None),
        P(("parts", "leaf"), None),
        P("parts", None),
    )
    return jax.shard_map(
        per_device,
        mesh=mesh,
        in_specs=placed,
        out_specs=P(("parts", "leaf"), None, None),
        check_vma=False,
    )
```

time: 549 us -> 226 us (0.41); the launches traced: 543 us -> 225 us
  matrix products: 207 us -> 4.58 us
  loops' own time: 149 us -> 0 us
  Pallas kernels: 0 us -> 96.6 us
  local copies, waits for them, and re-layouts: 132 us -> 40.4 us
  blocking collectives: 0 us -> 44.8 us
  starting transfers between devices: 24.1 us -> 6.55 us
  other arithmetic: 9.68 us -> 18.7 us
  waiting for transfers between devices: 6.79 us -> 0.02 us
    dot_general x41 -> x0, matrix products: 203 us -> none  [the longest x20 190 us: near_one(): jnp.einsum('snq,spq->np', sources[:, coords:], kernel, preferred_element_...]
    another operation x2 -> x0, loops' own time: 149 us -> none  [the longest x1 80.2 us: per_device(): far_terms = lax.map(far_one, leaf_ids)]
    pallas_call x0 -> x3, Pallas kernels: none -> 96.6 us  [the longest x2 76.2 us: sum_pairs(): pl.pallas_call(functools.partial(pair_kernel, rhs, base is not None), out...]
    all_gather x0 -> x1, blocking collectives: none -> 44.8 us  [per_device(): node_weights = lax.all_gather(partial_weights, 'leaf', axis=0)]
    dynamic_slice x80 -> x0, local copies, waits for them, and re-layouts: 26.5 us -> none  [the longest x40 25.6 us: per_device(): near_field = lax.map(near_one, leaf_ids)]
    slice x23 -> x1, local copies, waits for them, and re-layouts: 21.3 us -> 0.01 us  [per_device(): near_mask[:, :near_reach]]
    gather x2 -> x0, local copies, waits for them, and re-layouts: 20.9 us -> none  [the longest x1 14.2 us: per_device(): leaf_pack[lax.all_to_all(wanted, 'leaf', split_axis=0, concat_axis=0, til...]
    mul x40 -> x4, local copies, waits for them, and re-layouts: 26.8 us -> 5.96 us  [the longest x2 3.77 us: target_side(): ALPHA * jnp.sum(wide * wide, axis=1, keepdims=True)]
  transfers between devices with their start and end apart: 7 -> 3, of which waited for: 1 -> 0; matrix products, arithmetic and copies ran while one was open for 14% -> 26% of each run, Pallas kernels for 0% -> 22%
where the time goes in v1:
time: 226 us; the launch traced here: 225 us
  Pallas kernels  96.6 us (43%)
  blocking collectives  44.8 us (20%)
  local copies, waits for them, and re-layouts  40.4 us (18%)
  other arithmetic  18.7 us (8%)
  between operations  13.7 us (6%)
  starting transfers between devices  6.55 us (3%)
  matrix products  4.58 us (2%)
    pallas_call x2, Pallas kernels, sum_pairs(): pl.pallas_call(functools.partial(pair_kernel, rhs, base is not None), out...  76.2 us
    all_gather x1, blocking collectives, per_device(): node_weights = lax.all_gather(partial_weights, 'leaf', axis=0)  44.8 us
    pallas_call x1, Pallas kernels, per_device(): pl.pallas_call(functools.partial(far_kernel, rhs, near_reach, far_reach),...  20.4 us
    concatenate x6, local copies, waits for them, and re-layouts, target_side(): rows = jnp.concatenate([*cross, *norms, one, one, one, zero, zero], axis=1)  18.7 us
    another operation x6, other arithmetic  8.44 us
    unnamed x39, local copies, waits for them, and re-layouts  5.4 us
    ppermute x1, starting transfers between devices, with_halo(): before = lax.ppermute(last, axis, up)  4.63 us
  transfers between devices with their start and end apart: 3, of which 0 were waited for; matrix products, arithmetic and copies ran while one was open for 26% of the time, Pallas kernels for 22%

profile of v1, /device:TPU:1, one launch (start us, length us, event | category | flops | bytes accessed | tf_op | source)
XLA Modules:
  0.0 225.5 jit_solution(11384527453618653814)
XLA Ops:
  6.5 1.1 constant_dynamic-update-slice_fusion.1
  7.6 0.9 constant_dynamic-update-slice_fusion.pack_ref
  8.5 0.7 copy-done.9
  9.3 1.6 convolution_convert_fusion
  11.7 4.6 %collective-permute-start = (bf16[10,40,128]{2,1,0:T(8,128)(2,1)}, bf16[10,40,128]{2,1,0:T(8,128)(2,1)}, u32[]{:S(2)}, u32[]{:S(2)}) collective-permute-start(bf16[10,40,128]{2,1,0:T(8,128)(2,1)} %get-tuple-element.27), channel_id=1, source_target_pairs={{0,1},{1,2},{2,3},{3,4},{4,5},{5,6},{6,7},{7,8},{8,9},{9,10},{10,1... | collective-permute-start | bytes 307208 | tf_op jit(solution)/shard_map/ppermute | solution.py:25
  16.3 1.9 collective-permute-start.1
  18.7 44.8 %all-gather = f32[1024,128]{1,0:T(8,128)S(1)} all-gather(f32[32,128]{1,0:T(8,128)S(1)} %convolution_bitcast_fusion.1), channel_id=2, replica_groups=mesh['parts'=1,'leaf'=32] {'leaf'}, dimensions={0}, use_global_device_ids=true | all-gather | bytes 540672 | tf_op jit(solution)/shard_map/all_gather | solution.py:199
  63.5 1.2 gather_fusion
  67.2 2.3 copy.67
  69.4 2.5 %copy.68 = f32[20,1,256]{1,2,0:T(8,128)} copy(f32[20,1,256]{2,1,0:T(1,128)S(1)} %get-tuple-element.16) | data formatting | bytes 40960 | tf_op jit(solution)/shard_map/reduce_precision | solution.py:41
  72.7 1.6 copy.69
  74.4 1.5 copy.73
  75.9 1.5 copy.74
  77.4 1.5 copy.70
  81.4 2.9 %fusion.1 = (bf16[20,8,256]{1,2,0:T(8,128)(2,1)}, bf16[20,8,256]{1,2,0:T(8,128)(2,1)}, bf16[20,8,256]{1,2,0:T(8,128)(2,1)}) fusion(f32[20,8,256]{1,2,0:T(8,128)S(1)} %copy.64), kind=kLoop, calls=%fused_computation.9 | loop fusion | flops 327680 | bytes 409600 | tf_op jit(solution)/shard_map/convert.10
  84.2 1.0 copy-done.2
  85.3 2.3 %fusion.3 = (bf16[20,1,256]{1,2,0:T(8,128)(2,1)}, bf16[20,1,256]{1,2,0:T(8,128)(2,1)}) fusion(f32[20,1,256]{1,2,0:T(8,128)S(1)} %copy-done.1, f32[20,1,256]{1,2,0:T(8,128)S(1)} %copy-done.2), kind=kLoop, calls=%fused_computation.11 | loop fusion | flops 30720 | bytes 61440 | tf_op jit(solution)/shard_map/convert.13
  87.8 1.4 concatenate.42
  89.2 10.6 %concatenate.43 = bf16[20,32,256]{1,2,0:T(8,128)(2,1)} concatenate(bf16[20,8,256]{1,2,0:T(8,128)(2,1)} %get-tuple-element.23, bf16[20,8,256]{1,2,0:T(8,128)(2,1)} %get-tuple-element.22, bf16[20,8,256]{1,2,0:T(8,128)(2,1)} %get-tuple-element.21, bf16[20,1,256]{1,2,0:T(8,128)(2,1)} %copy.69, bf16[20,1,256]{1,2,0:T(8,128)(2,1)} %get-tuple-element.18, ...), dimensions={1} | concatenate | bytes 655360 | tf_op jit(solution)/shard_map/concatenate | solution.py:60
  99.8 1.8 fusion.7
  102.3 1.5 fusion.9
  104.0 0.8 copy-done.7
  105.0 6.2 %concatenate.47 = bf16[20,32,128]{1,2,0:T(8,128)(2,1)} concatenate(bf16[20,8,128]{1,2,0:T(8,128)(2,1)} %get-tuple-element.26, bf16[20,8,128]{1,2,0:T(8,128)(2,1)S(1)} %copy-done.8, bf16[20,8,128]{1,2,0:T(8,128)(2,1)S(1)} %copy-done.7, bf16[20,1,128]{1,2,0:T(8,128)(2,1)S(1)} %copy.75, bf16[20,1,128]{1,2,0:T(8,128)(2,1)} %get-tuple-element.20, ...), dimensions={1} | concatenate | bytes 327680 | tf_op jit(solution)/shard_map/concatenate | solution.py:60
  111.9 1.2 fusion.71.scale_ref
  113.9 0.9 select_reduce_fusion.3
  115.0 1.3 select_reduce_fusion
  116.3 2.7 %fusion.10.expansion_ref = bf16[32,128]{1,0:T(8,128)(2,1)} fusion(f32[8,32,128]{2,1,0:T(8,128)} %gather_fusion, f32[8,128]{1,0:T(8,128)S(1)} %bitcast.60, f32[128]{0:T(128)S(1)} %get-tuple-element.44, f32[8,128]{1,0:T(8,128)S(1)} %bitcast.59, f32[128]{0:T(128)S(1)} %get-tuple-element.45, f32[8,128]{1,0:T(8,128)S(1)} %bitcast.58, ...), kind=kOutput, calls=%fused_computation.32 | convolution fusion | flops 53874688 | bytes 176128 | tf_op jit(solution)/shard_map/mrs,mns->nr/dot_general | solution.py:205
  119.0 30.2 %own_pairs.1.base_ref = f32[20,32,256]{2,1,0:T(8,128)} custom-call(s32[1]{0:T(128)} %bitcast.25.count_ref, s32[304]{0:T(512)} %get-tuple-element.8.source_ref, s32[304]{0:T(512)} %get-tuple-element.7.target_ref, f32[304]{0:T(512)} %fusion.71.scale_ref, bf16[20,256,32]{2,1,0:T(8,128)(2,1)} %bitcast.51, bf16[20,40,256]{2,1,0:T(8,128)(2,1)} %copy-done.9), custom_call_target="tpu_custom_call" | custom-call | flops 2550136832 | bytes 409600 | tf_op jit(solution)/shard_map/own_pairs/pallas_call | solution.py:120
  149.2 1.2 fusion.70.scale_ref
  150.5 1.7 pad_maximum_fusion.pack_ref
  152.2 20.4 %far_field.1.rest_0_ = f32[20,32,256]{2,1,0:T(8,128)} custom-call(s32[20,6]{1,0:T(8,128)} %copy.78.mask_ref, bf16[20,128,32]{2,1,0:T(8,128)(2,1)} %bitcast.49, bf16[40,40,128]{2,1,0:T(8,128)(2,1)} %pad_maximum_fusion.pack_ref, bf16[20,128,128]{2,1,0:T(8,128)(2,1)} %transfer_ref.1, bf16[32,128]{1,0:T(8,128)(2,1)} %fusion.10.expansion_ref, ...), custom_call_target="tpu_custom_call" | custom-call | tf_op jit(solution)/shard_map/far_field/pallas_call | solution.py:232
  172.6 46.0 %other_pairs.1 = f32[20,32,256]{2,1,0:T(8,128)} custom-call(s32[1]{0:T(128)} %bitcast.count_ref, s32[544]{0:T(1024)} %get-tuple-element.6.source_ref, s32[544]{0:T(1024)} %get-tuple-element.5.target_ref, f32[544]{0:T(1024)} %fusion.70.scale_ref, bf16[20,256,32]{2,1,0:T(8,128)(2,1)} %bitcast.52, bf16[640,40,256]{2,1,0:T(8,128)(2,1)} %all-gather.3.cloned.1.call-done.pack_ref, ...), custom_call_target="tpu_custom_call" | custom-call | flops 4563402752 | bytes 13107200 | tf_op jit(solution)/shard_map/other_pairs/pallas_call | solution.py:120
  (84 shorter events, 9.9 us)
Async XLA Ops:
  6.5 11.7 %copy-start = (s32[16,8]{0,1:T(8,128)S(1)}, s32[16,8]{0,1:T(8,128)}, u32[]{:S(2)}) copy-start(s32[16,8]{0,1:T(8,128)} %param.21) | copy-start | bytes 1540
  6.5 2.8 %copy-start.10 = (bf16[20,32,256]{2,1,0:T(8,128)(2,1)S(1)}, bf16[20,32,256]{2,1,0:T(8,128)(2,1)}, u32[]{:S(2)}) copy-start(bf16[20,32,256]{2,1,0:T(8,128)(2,1)} %param.12) | copy-start | bytes 983044
  6.5 166.0 %all-gather.3.cloned.1.call-start = ((), (), s32[]{:S(2)}) async-start(), calls=%async_computation | async-start | bytes 13516800 | tf_op jit(solution)/shard_map/all_gather | solution.py:187
  7.6 3.4 %copy-start.11 = (bf16[20,8,128]{2,1,0:T(8,128)(2,1)S(1)}, bf16[20,8,128]{2,1,0:T(8,128)(2,1)}, u32[]{:S(2)}) copy-start(bf16[20,8,128]{2,1,0:T(8,128)(2,1)} %param.15) | copy-start | bytes 122884
  8.5 0.8 copy-start.9
  8.5 9.9 %copy-start.6 = (bf16[20,128,128]{2,1,0:T(8,128)(2,1)S(1)}, bf16[20,128,128]{2,1,0:T(8,128)(2,1)}, u32[]{:S(2)}) copy-start(bf16[20,128,128]{2,1,0:T(8,128)(2,1)} %transfer_ref.1) | copy-start | bytes 1966084
  11.7 53.1 %copy-start.13 = (bf16[16,8,128]{2,1,0:T(8,128)(2,1)S(1)}, bf16[16,8,128]{2,1,0:T(8,128)(2,1)}, u32[]{:S(2)}) copy-start(bf16[16,8,128]{2,1,0:T(8,128)(2,1)} %param.16) | copy-start | bytes 98308
  11.7 53.7 %copy-start.15 = (s32[20,14]{0,1:T(8,128)S(1)}, s32[20,14]{0,1:T(8,128)}, u32[]{:S(2)}) copy-start(s32[20,14]{0,1:T(8,128)} %param.17) | copy-start | bytes 3364
  11.7 138.8 %collective-permute-start = (bf16[10,40,128]{2,1,0:T(8,128)(2,1)}, bf16[10,40,128]{2,1,0:T(8,128)(2,1)}, u32[]{:S(2)}, u32[]{:S(2)}) collective-permute-start(bf16[10,40,128]{2,1,0:T(8,128)(2,1)} %get-tuple-element.27), channel_id=1, source_target_pairs={{0,1},{1,2},{2,3},{3,4},{4,5},{5,6},{6,7},{7,8},{8,9},{9,10},{10,1... | collective-permute-start | bytes 307208 | tf_op jit(solution)/shard_map/ppermute | solution.py:25
  16.3 134.1 %collective-permute-start.1 = (bf16[10,40,128]{2,1,0:T(8,128)(2,1)}, bf16[10,40,128]{2,1,0:T(8,128)(2,1)}, u32[]{:S(2)}, u32[]{:S(2)}) collective-permute-start(bf16[10,40,128]{2,1,0:T(8,128)(2,1)} %get-tuple-element.28), channel_id=1, source_target_pairs={{1,0},{2,1},{3,2},{4,3},{5,4},{6,5},{7,6},{8,7},{9,8},{10,9},{11,1... | collective-permute-start | bytes 307208 | tf_op jit(solution)/shard_map/ppermute | solution.py:26
  18.2 48.8 %copy-start.12 = (bf16[20,8,256]{2,1,0:T(8,128)(2,1)S(1)}, bf16[20,8,256]{2,1,0:T(8,128)(2,1)}, u32[]{:S(2)}) copy-start(bf16[20,8,256]{2,1,0:T(8,128)(2,1)} %param.11) | copy-start | bytes 245764
  77.4 1.9 copy-start.16
  77.4 2.9 %copy-start.14 = (s32[20,12]{0,1:T(8,128)S(1)}, s32[20,12]{0,1:T(8,128)}, u32[]{:S(2)}) copy-start(s32[20,12]{0,1:T(8,128)} %param.19) | copy-start | bytes 2884
  81.3 2.9 %copy-start.1 = (f32[20,1,256]{1,2,0:T(8,128)S(1)}, f32[20,1,256]{1,2,0:T(8,128)}, u32[]{:S(2)}) copy-start(f32[20,1,256]{1,2,0:T(8,128)} %copy.67) | copy-start | bytes 61444
  81.3 3.9 %copy-start.2 = (f32[20,1,256]{1,2,0:T(8,128)S(1)}, f32[20,1,256]{1,2,0:T(8,128)}, u32[]{:S(2)}) copy-start(f32[20,1,256]{1,2,0:T(8,128)} %copy.68) | copy-start | bytes 61444
  89.2 10.6 %copy-start.3 = (f32[20,8,128]{1,2,0:T(8,128)S(1)}, f32[20,8,128]{1,2,0:T(8,128)}, u32[]{:S(2)}) copy-start(f32[20,8,128]{1,2,0:T(8,128)} %copy.70) | copy-start | bytes 245764
  99.8 1.8 copy-start.4
  99.8 2.4 %copy-start.5 = (f32[20,1,128]{1,2,0:T(8,128)S(1)}, f32[20,1,128]{1,2,0:T(8,128)}, u32[]{:S(2)}) copy-start(f32[20,1,128]{1,2,0:T(8,128)} %copy.74) | copy-start | bytes 30724
  103.7 1.1 copy-start.7
  103.7 1.3 copy-start.8
  105.0 8.7 %copy-start.17 = (pred[300]{0:T(512)(128)(4,1)S(1)}, pred[300]{0:T(512)(128)(4,1)}, u32[]{:S(2)}) copy-start(pred[300]{0:T(512)(128)(4,1)} %ne.32) | copy-start | bytes 904
Sparse Core Ops, SparseCore 0:
  10.2 103.4 all-gather.2

commit v2 on v1

--- a/solution.py
+++ b/solution.py
@@ -37,10 +37,6 @@
     return (1.0 + scaled) * jnp.exp(-scaled)
 
 
-def reduced(value):
-    return lax.reduce_precision(value, 8, 7)
-
-
 def rounded(value):
     return value.astype(jnp.bfloat16).astype(jnp.float32)
 
@@ -52,13 +48,41 @@
 
 
 def target_side(points):
-    wide = points.astype(jnp.float32)
-    cross = three_parts(-2.0 * ALPHA * wide, reduced)
-    norms = three_parts(ALPHA * jnp.sum(wide * wide, axis=1, keepdims=True), reduced)
-    one = jnp.ones_like(norms[0])
-    zero = jnp.zeros_like(one)
-    rows = jnp.concatenate([*cross, *norms, one, one, one, zero, zero], axis=1)
-    return jnp.swapaxes(rows.astype(jnp.bfloat16), 1, 2)
+    cross = three_parts(-2.0 * ALPHA * points, rounded)
+    high, middle, low = three_parts(
+        ALPHA * jnp.sum(points * points, axis=0, keepdims=True), rounded
+    )
+    row = lax.broadcasted_iota(jnp.int32, points.shape, 0)
+    tail = jnp.where(
+        row == 0,
+        high,
+        jnp.where(row == 1, middle, jnp.where(row == 2, low, jnp.where(row < 6, 1.0, 0.0))),
+    )
+    return jnp.concatenate([*cross, tail], axis=0).T.astype(jnp.bfloat16)
+
+
+def sides_kernel(points_ref, skeleton_ref, points_side_ref, skeleton_side_ref):
+    def one(leaf, carry):
+        points_side_ref[leaf] = target_side(points_ref[leaf].astype(jnp.float32))
+        skeleton_side_ref[leaf] = target_side(skeleton_ref[leaf].astype(jnp.float32))
+        return carry
+
+    lax.fori_loop(0, points_ref.shape[0], one, 0)
+
+
+def target_sides(*clouds):
+    vectors = pl.BlockSpec(memory_space=pltpu.VMEM)
+    return pl.pallas_call(
+        sides_kernel,
+        out_shape=[
+            jax.ShapeDtypeStruct((c.shape[0], c.shape[2], 4 * c.shape[1]), jnp.bfloat16)
+            for c in clouds
+        ],
+        in_specs=[vectors] * 2,
+        out_specs=[vectors] * 2,
+        compiler_params=pltpu.CompilerParams(vmem_limit_bytes=VMEM_LIMIT),
+        name="target_sides",
+    )(*clouds)
 
 
 def source_side(points):
@@ -116,16 +140,13 @@
     scalars = pl.BlockSpec(memory_space=pltpu.SMEM)
     vectors = pl.BlockSpec(memory_space=pltpu.VMEM)
     extra = [] if base is None else [base]
-    work = pairs[1].shape[0] * length * pack.shape[2]
     return pl.pallas_call(
         functools.partial(pair_kernel, rhs, base is not None),
         out_shape=jax.ShapeDtypeStruct((leaves, rhs, length), jnp.float32),
         in_specs=[scalars] * 4 + [vectors] * (2 + len(extra)),
         out_specs=vectors,
         compiler_params=pltpu.CompilerParams(vmem_limit_bytes=VMEM_LIMIT),
-        cost_estimate=pl.CostEstimate(
-            flops=2 * work * 64, bytes_accessed=2 * pack.size, transcendentals=2 * work
-        ),
+        cost_estimate=pl.CostEstimate(flops=1024, bytes_accessed=1024, transcendentals=0),
         name=name,
     )(*pairs, side, pack, *extra)
 
@@ -194,18 +215,6 @@
     partial_weights = jnp.einsum(
         "lrs,lnr->ns", transfer, weights, preferred_element_type=jnp.float32
     )
-    per_node = devices // node_count
-    own_node = device // per_node
-    node_weights = lax.all_gather(partial_weights, "leaf", axis=0)
-    node_weights = node_weights.reshape((node_count, per_node) + partial_weights.shape).sum(axis=1)
-    far_nodes = top_far[own_node]
-    node_kernel = matern(
-        top_skeleton[own_node].astype(jnp.float32), top_skeleton[far_nodes].astype(jnp.float32)
-    )
-    expansion = jnp.einsum(
-        "mrs,mns->nr", node_kernel, node_weights[far_nodes], precision=lax.Precision.HIGHEST
-    ).astype(jnp.bfloat16)
-
     leaf_ids = jnp.arange(local_count, dtype=jnp.int32)
     reach = jnp.arange(-near_reach, near_reach + 1, dtype=jnp.int32)
     window = leaf_ids[:, None] + reach[None, :]
@@ -225,8 +234,21 @@
         jnp.broadcast_to(leaf_ids[:, None], (local_count, window.shape[1] + remote.shape[1])),
     )
 
-    side = target_side(points)
+    side, far_side = target_sides(points, skeleton)
     own_field = sum_pairs(own_pairs, side, leaf_pack, name="own_pairs")
+    partial_weights, own_field = lax.optimization_barrier((partial_weights, own_field))
+    per_node = devices // node_count
+    own_node = device // per_node
+    node_weights = lax.all_gather(partial_weights, "leaf", axis=0)
+    node_weights = node_weights.reshape((node_count, per_node) + partial_weights.shape).sum(axis=1)
+    far_nodes = top_far[own_node]
+    node_kernel = matern(
+        top_skeleton[own_node].astype(jnp.float32), top_skeleton[far_nodes].astype(jnp.float32)
+    )
+    expansion = jnp.einsum(
+        "mrs,mns->nr", node_kernel, node_weights[far_nodes], precision=lax.Precision.HIGHEST
+    ).astype(jnp.bfloat16)
+
     scalars = pl.BlockSpec(memory_space=pltpu.SMEM)
     vectors = pl.BlockSpec(memory_space=pltpu.VMEM)
     with_far = pl.pallas_call(
@@ -236,7 +258,7 @@
         out_specs=vectors,
         compiler_params=pltpu.CompilerParams(vmem_limit_bytes=VMEM_LIMIT),
         name="far_field",
-    )(far_mask, target_side(skeleton), far_wide, transfer, expansion, basis, own_field)
+    )(far_mask, far_side, far_wide, transfer, expansion, basis, own_field)
     return sum_pairs(other_pairs, side, gathered, with_far, name="other_pairs")
 
 

time: 226 us -> 181 us (0.80)
  local copies, waits for them, and re-layouts: 40.4 us -> 5.75 us
  other arithmetic: 18.7 us -> 7.25 us
  Pallas kernels: 96.6 us -> 99.8 us
    concatenate x6 -> x0, local copies, waits for them, and re-layouts: 18.7 us -> none  [target_side(): rows = jnp.concatenate([*cross, *norms, one, one, one, zero, zero], axis=1)]
    another operation x6 -> x0, other arithmetic: 8.44 us -> none
    mul x4 -> x0, local copies, waits for them, and re-layouts: 5.96 us -> none  [the longest x2 3.77 us: target_side(): ALPHA * jnp.sum(wide * wide, axis=1, keepdims=True)]
    pallas_call x0 -> x1, Pallas kernels: none -> 4.46 us  [target_sides(): pl.pallas_call(sides_kernel, out_shape=[jax.ShapeDtypeStruct((c.shape[0],...]
    reduce_precision x2 -> x0, local copies, waits for them, and re-layouts: 4.05 us -> none  [reduced(): return lax.reduce_precision(value, 8, 7)]
    unnamed x39 -> x25, local copies, waits for them, and re-layouts: 5.4 us -> 2.67 us
  transfers between devices with their start and end apart: 3 -> 3, of which waited for: 0 -> 0; matrix products, arithmetic and copies ran while one was open for 26% -> 8% of each run, Pallas kernels for 22% -> 30%
where the time goes in v2:
time: 181 us
  Pallas kernels  99.8 us (55%)
  blocking collectives  44.6 us (25%)
  between operations  13.7 us (8%)
  other arithmetic  7.25 us (4%)
  starting transfers between devices  6.56 us (4%)
  local copies, waits for them, and re-layouts  5.75 us (3%)
  matrix products  3.67 us (2%)
    pallas_call x2, Pallas kernels, sum_pairs(): pl.pallas_call(functools.partial(pair_kernel, rhs, base is not None), out...  74.8 us
    all_gather x1, blocking collectives, per_device(): node_weights = lax.all_gather(partial_weights, 'leaf', axis=0)  44.6 us
    pallas_call x1, Pallas kernels, per_device(): pl.pallas_call(functools.partial(far_kernel, rhs, near_reach, far_reach),...  20.5 us
    ppermute x1, starting transfers between devices, with_halo(): before = lax.ppermute(last, axis, up)  4.64 us
    pallas_call x1, Pallas kernels, target_sides(): pl.pallas_call(sides_kernel, out_shape=[jax.ShapeDtypeStruct((c.shape[0],...  4.46 us
  transfers between devices with their start and end apart: 3, of which 0 were waited for; matrix products, arithmetic and copies ran while one was open for 8% of the time, Pallas kernels for 30%

profile of v2, /device:TPU:1, one launch (start us, length us, event | category | flops | bytes accessed | tf_op | source)
XLA Modules:
  0.0 181.3 jit_solution(3520756450733081442)
XLA Ops:
  6.5 1.1 constant_dynamic-update-slice_fusion.1
  7.6 0.9 constant_dynamic-update-slice_fusion.pack_ref
  8.5 0.8 copy-done.1
  9.3 1.6 convolution_convert_fusion
  11.0 4.6 %collective-permute-start = (bf16[10,40,128]{2,1,0:T(8,128)(2,1)S(1)}, bf16[10,40,128]{2,1,0:T(8,128)(2,1)S(1)}, u32[]{:S(2)}, u32[]{:S(2)}) collective-permute-start(bf16[10,40,128]{2,1,0:T(8,128)(2,1)S(1)} %get-tuple-element.21), channel_id=1, source_target_pairs={{0,1},{1,2},{2,3},{3,4},{4,5},{5,6},{6,7},{7,8},{8,9},{9,10},{10,1... | collective-permute-start | bytes 307208 | tf_op jit(solution)/shard_map/ppermute | solution.py:25
  15.7 1.9 %collective-permute-start.1 = (bf16[10,40,128]{2,1,0:T(8,128)(2,1)S(1)}, bf16[10,40,128]{2,1,0:T(8,128)(2,1)S(1)}, u32[]{:S(2)}, u32[]{:S(2)}) collective-permute-start(bf16[10,40,128]{2,1,0:T(8,128)(2,1)S(1)} %get-tuple-element.22), channel_id=1, source_target_pairs={{1,0},{2,1},{3,2},{4,3},{5,4},{6,5},{7,6},{8,7},{9,8},{10,9},{11,1... | collective-permute-start | bytes 307208 | tf_op jit(solution)/shard_map/ppermute | solution.py:26
  17.6 4.5 %target_sides.1 = (bf16[20,256,32]{2,1,0:T(8,128)(2,1)}, bf16[20,128,32]{2,1,0:T(8,128)(2,1)}) custom-call(bf16[20,8,256]{2,1,0:T(8,128)(2,1)} %points_ref.1, bf16[20,8,128]{2,1,0:T(8,128)(2,1)} %skeleton_ref.1), custom_call_target="tpu_custom_call" | custom-call | tf_op jit(solution)/shard_map/target_sides/pallas_call | solution.py:75
  22.1 0.7 convert_reduce_fusion.1
  22.9 0.1 copy.25
  23.0 0.1 ne.30
  23.2 0.1 add.149
  23.3 1.2 fusion.61.scale_ref
  24.5 0.2 select_reduce_fusion.5
  24.6 0.9 select_reduce_fusion.3
  25.5 29.0 %own_pairs.1.base_ref = f32[20,32,256]{2,1,0:T(8,128)} custom-call(s32[1]{0:T(128)} %bitcast.2.count_ref, s32[304]{0:T(512)} %get-tuple-element.16.source_ref, s32[304]{0:T(512)} %get-tuple-element.15.target_ref, f32[304]{0:T(512)} %fusion.61.scale_ref, bf16[20,256,32]{2,1,0:T(8,128)(2,1)} %get-tuple-element.9.side_ref, bf16[20,40,256]{2,1,0:T(8,128)(2,1)} %copy-done.1), custom_call_target="tpu_custom_call" | custom-call | flops 1024 | bytes 1024 | tf_op jit(solution)/shard_map/own_pairs/pallas_call | solution.py:143
  54.6 0.2 convolution_bitcast_fusion.1
  54.8 0.2 dynamic-slice_reduce_fusion
  55.0 44.6 %all-gather = f32[1024,128]{1,0:T(8,128)S(1)} all-gather(f32[32,128]{1,0:T(8,128)S(1)} %convolution_bitcast_fusion.1), channel_id=2, replica_groups=mesh['parts'=1,'leaf'=32] {'leaf'}, dimensions={0}, use_global_device_ids=true | all-gather | bytes 540672 | tf_op jit(solution)/shard_map/all_gather | solution.py:242
  99.6 0.6 gather_fusion
  100.2 0.6 gather_fusion.1
  100.8 0.7 copy.27.mask_ref
  101.6 0.1 copy.28
  101.7 0.1 and.82
  101.8 0.1 copy.24
  102.1 0.7 convert_reduce_fusion
  102.8 0.2 select_reduce_fusion.2
  103.0 1.3 select_reduce_fusion
  104.3 1.8 %fusion.2.expansion_ref = bf16[32,128]{1,0:T(8,128)(2,1)} fusion(f32[8,32,128]{2,1,0:T(8,128)S(1)} %gather_fusion, f32[8,128]{1,0:T(8,128)S(1)} %bitcast.51, f32[128]{0:T(128)S(1)} %get-tuple-element.34, f32[8,128]{1,0:T(8,128)S(1)} %bitcast.50, f32[128]{0:T(128)S(1)} %get-tuple-element.35, f32[8,128]{1,0:T(8,128)S(1)} %bitcast.49, ...), kind=kOutput, calls=%fused_computation.12 | convolution fusion | flops 53874688 | bytes 176128 | tf_op jit(solution)/shard_map/mrs,mns->nr/dot_general | solution.py:248
  106.1 1.2 fusion.60.scale_ref
  107.3 0.8 pad_maximum_fusion.pack_ref
  108.1 20.5 %far_field.1.rest_0_ = f32[20,32,256]{2,1,0:T(8,128)} custom-call(s32[20,6]{1,0:T(8,128)} %copy.27.mask_ref, bf16[20,128,32]{2,1,0:T(8,128)(2,1)} %get-tuple-element.10.side_ref, bf16[40,40,128]{2,1,0:T(8,128)(2,1)} %pad_maximum_fusion.pack_ref, bf16[20,128,128]{2,1,0:T(8,128)(2,1)} %transfer_ref.1, bf16[32,128]{1,0:T(8,128)(2,1)} %fusion.2.expansion_ref, ...), custom_call_target="tpu_custom_call" | custom-call | tf_op jit(solution)/shard_map/far_field/pallas_call | solution.py:254
  128.6 45.8 %other_pairs.1 = f32[20,32,256]{2,1,0:T(8,128)} custom-call(s32[1]{0:T(128)} %bitcast.count_ref, s32[544]{0:T(1024)} %get-tuple-element.14.source_ref, s32[544]{0:T(1024)} %get-tuple-element.13.target_ref, f32[544]{0:T(1024)} %fusion.60.scale_ref, bf16[20,256,32]{2,1,0:T(8,128)(2,1)} %get-tuple-element.9.side_ref, ...), custom_call_target="tpu_custom_call" | custom-call | flops 1024 | bytes 1024 | tf_op jit(solution)/shard_map/other_pairs/pallas_call | solution.py:143
  (47 shorter events, 0.6 us)
Async XLA Ops:
  6.5 48.3 %copy-start = (s32[16,8]{0,1:T(8,128)S(1)}, s32[16,8]{0,1:T(8,128)}, u32[]{:S(2)}) copy-start(s32[16,8]{0,1:T(8,128)} %param.21) | copy-start | bytes 1540
  6.5 2.8 %copy-start.3 = (bf16[20,32,256]{2,1,0:T(8,128)(2,1)S(1)}, bf16[20,32,256]{2,1,0:T(8,128)(2,1)}, u32[]{:S(2)}) copy-start(bf16[20,32,256]{2,1,0:T(8,128)(2,1)} %param.12) | copy-start | bytes 983044
  6.5 4.4 %copy-start.4 = (bf16[20,8,128]{2,1,0:T(8,128)(2,1)S(1)}, bf16[20,8,128]{2,1,0:T(8,128)(2,1)}, u32[]{:S(2)}) copy-start(bf16[20,8,128]{2,1,0:T(8,128)(2,1)} %skeleton_ref.1) | copy-start | bytes 122884
  6.5 122.1 %all-gather.3.cloned.1.call-start = ((), (), s32[]{:S(2)}) async-start(), calls=%async_computation | async-start | bytes 13516800 | tf_op jit(solution)/shard_map/all_gather | solution.py:208
  8.5 0.8 copy-start.1
  8.5 13.6 %copy-start.9 = (s32[20,14]{0,1:T(8,128)S(1)}, s32[20,14]{0,1:T(8,128)}, u32[]{:S(2)}) copy-start(s32[20,14]{0,1:T(8,128)} %param.17) | copy-start | bytes 3364
  11.0 43.6 %copy-start.2 = (bf16[20,128,128]{2,1,0:T(8,128)(2,1)S(1)}, bf16[20,128,128]{2,1,0:T(8,128)(2,1)}, u32[]{:S(2)}) copy-start(bf16[20,128,128]{2,1,0:T(8,128)(2,1)} %transfer_ref.1) | copy-start | bytes 1966084
  11.0 96.3 %collective-permute-start = (bf16[10,40,128]{2,1,0:T(8,128)(2,1)S(1)}, bf16[10,40,128]{2,1,0:T(8,128)(2,1)S(1)}, u32[]{:S(2)}, u32[]{:S(2)}) collective-permute-start(bf16[10,40,128]{2,1,0:T(8,128)(2,1)S(1)} %get-tuple-element.21), channel_id=1, source_target_pairs={{0,1},{1,2},{2,3},{3,4},{4,5},{5,6},{6,7},{7,8},{8,9},{9,10},{10,1... | collective-permute-start | bytes 307208 | tf_op jit(solution)/shard_map/ppermute | solution.py:25
  15.7 91.7 %collective-permute-start.1 = (bf16[10,40,128]{2,1,0:T(8,128)(2,1)S(1)}, bf16[10,40,128]{2,1,0:T(8,128)(2,1)S(1)}, u32[]{:S(2)}, u32[]{:S(2)}) collective-permute-start(bf16[10,40,128]{2,1,0:T(8,128)(2,1)S(1)} %get-tuple-element.22), channel_id=1, source_target_pairs={{1,0},{2,1},{3,2},{4,3},{5,4},{6,5},{7,6},{8,7},{9,8},{10,9},{11,1... | collective-permute-start | bytes 307208 | tf_op jit(solution)/shard_map/ppermute | solution.py:26
  54.5 45.7 %copy-start.6 = (bf16[16,8,128]{2,1,0:T(8,128)(2,1)S(1)}, bf16[16,8,128]{2,1,0:T(8,128)(2,1)}, u32[]{:S(2)}) copy-start(bf16[16,8,128]{2,1,0:T(8,128)(2,1)} %param.16) | copy-start | bytes 98308
  54.6 46.2 %copy-start.10 = (s32[20,6]{0,1:T(8,128)S(1)}, s32[20,6]{0,1:T(8,128)}, u32[]{:S(2)}) copy-start(s32[20,6]{0,1:T(8,128)} %param.20) | copy-start | bytes 1444
  54.6 47.2 %copy-start.7 = (s32[20,12]{0,1:T(8,128)S(1)}, s32[20,12]{0,1:T(8,128)}, u32[]{:S(2)}) copy-start(s32[20,12]{0,1:T(8,128)} %param.19) | copy-start | bytes 2884
  54.6 47.2 %copy-start.8 = (s32[20,12]{0,1:T(8,128)S(1)}, s32[20,12]{0,1:T(8,128)}, u32[]{:S(2)}) copy-start(s32[20,12]{0,1:T(8,128)} %param.18) | copy-start | bytes 2884
  104.3 3.1 %copy-start.5 = (bf16[20,8,128]{2,1,0:T(8,128)(2,1)S(1)}, bf16[20,8,128]{2,1,0:T(8,128)(2,1)}, u32[]{:S(2)}) copy-start(bf16[20,8,128]{2,1,0:T(8,128)(2,1)} %skeleton_ref.1) | copy-start | bytes 122884
Sparse Core Ops, SparseCore 0:
  10.2 104.2 all-gather.2
